TPU v7x, 256 devices: a whole 4x4x8 slice. The times are simulated.
256 devices in a mesh: space: 16 (over y, z_lo), vel: 16 (over x, z_hi, core).
Axes of the slice: x: 4, y: 4, z: 8 (z_hi: 2, z_lo: 4; z = z_hi * 4 + z_lo), core: 2. Of those that a mesh axis runs over, the one named last changes fastest.
Arguments:
- distribution: float32 [13824, 64, 128], P('vel', 'space'), as said below
- wall_mask: int32 [64, 128], P('space'), may hold values from 0 to 1, as said below
Outputs:
- evolved: float32 [13824, 64, 128], P('vel', 'space')
Inputs may be any that keep to these rules, and one draw needn't show every extreme that they name: `wall_mask`: the cells with 1 are those of two neighbouring x layers p and p + 1 (p + 1 taken modulo 64) over one run of y cells, for one p. `distribution`: every entry is nonnegative.
All inputs are finite; a program needn't handle non-finite values.
Results may differ from a plain program's by a relative error of at most 0.0003.
Values sent between devices are 32-bit elements; how exact they have to be, the bound alone decides.
A program may use at most 64 MiB of HBM per device.

v0:
```python
import math

import jax
import jax.numpy as jnp
from jax import lax
from jax.sharding import PartitionSpec as P

NODES = 24
STEPS = 2


half_span = 4.5
step_ratio = 0.1
knudsen = 0.5
prandtl = 2.0 / 3.0
omega_exp = 0.81
dens_floor = 0.1
temp_floor = 0.1


def with_halo(cells, sides, width):
    for axis, dim in sides:
        count = lax.axis_size(axis)
        head = lax.slice_in_dim(cells, 0, width, axis=dim)
        tail = lax.slice_in_dim(cells, cells.shape[dim] - width, cells.shape[dim], axis=dim)
        cells = jnp.concatenate(
            [
                lax.ppermute(tail, axis, [(i, (i + 1) % count) for i in range(count)]),
                cells,
                lax.ppermute(head, axis, [((i + 1) % count, i) for i in range(count)]),
            ],
            axis=dim,
        )
    return cells


def swapped(block, axis, apart):
    count = lax.axis_size(axis)
    route = []
    for low in range(count):
        high = low | 1 << apart
        if high != low and high < count:
            route += [(low, high), (high, low)]
    return lax.ppermute(block, axis, route)


def velocity_nodes(first, count, nodes):
    index = first + jnp.arange(count, dtype=jnp.int32)
    total = nodes**3
    plane = nodes * nodes
    upper = index >= total // 2
    folded = jnp.where(upper, total - 1 - index, index)
    xcell = folded // plane
    xcell = jnp.where(upper, nodes - 1 - xcell, xcell)
    rest = folded % plane
    ycell = rest // nodes
    zcell = rest % nodes
    spacing = 2.0 * half_span / nodes
    return tuple(
        ((cell.astype(jnp.float32) + 0.5) * spacing - half_span for cell in (xcell, ycell, zcell))
    )


def moment_table(vx, vy, vz, nodes):
    weight = (2.0 * half_span / nodes) ** 3 / (2.0 * math.pi) ** 1.5
    square = vx * vx + vy * vy + vz * vz
    rows = [
        jnp.ones_like(vx),
        vx,
        vy,
        vz,
        vx * vx,
        vy * vy,
        vz * vz,
        vx * vy,
        vx * vz,
        vy * vz,
        vx * square,
        vy * square,
        vz * square,
    ]
    return jnp.stack(rows) * weight


def shakhov_params(moments):
    raw = moments[0]
    density = jnp.maximum(raw, dens_floor)
    mx, my, mz = (moments[1], moments[2], moments[3])
    ux, uy, uz = (mx / density, my / density, mz / density)
    sxx, syy, szz = (moments[4], moments[5], moments[6])
    sxy, sxz, syz = (moments[7], moments[8], moments[9])
    energy = sxx + syy + szz
    speed2 = ux * ux + uy * uy + uz * uz
    temper = jnp.maximum((energy / density - speed2) / 3.0, temp_floor)
    along = ux * mx + uy * my + uz * mz

    def heat(third, first, uval, dot_row):
        return 0.5 * (
            third
            - 2.0 * dot_row
            + speed2 * first
            - uval * energy
            + 2.0 * uval * along
            - uval * speed2 * raw
        )

    qx = heat(moments[10], mx, ux, ux * sxx + uy * sxy + uz * sxz)
    qy = heat(moments[11], my, uy, ux * sxy + uy * syy + uz * syz)
    qz = heat(moments[12], mz, uz, ux * sxz + uy * syz + uz * szz)
    factor = step_ratio * density * temper ** (1.0 - omega_exp) / knudsen
    return jnp.stack([density, ux, uy, uz, temper, qx, qy, qz, factor])


def relax(field, params, vx, vy, vz):
    shape = (9,) + field.shape[1:]
    density, ux, uy, uz, temper, qx, qy, qz, factor = params.reshape(shape)
    cx = vx[:, None, None] - ux[None]
    cy = vy[:, None, None] - uy[None]
    cz = vz[:, None, None] - uz[None]
    square = cx * cx + cy * cy + cz * cz
    maxwell = density[None] * temper[None] ** (-1.5) * jnp.exp(-square / (2.0 * temper[None]))
    flux = (cx * qx[None] + cy * qy[None] + cz * qz[None]) / (
        5.0 * density[None] * temper[None] * temper[None]
    )
    shakhov = maxwell * (1.0 + (1.0 - prandtl) * flux * (square / temper[None] - 5.0))
    return field + factor[None] * (shakhov - field)


def upwind_y(field, speed):
    back_one = jnp.roll(field, 1, 2)
    back_two = jnp.roll(field, 2, 2)
    fore_one = jnp.roll(field, -1, 2)
    fore_two = jnp.roll(field, -2, 2)
    plus = 0.5 * (3.0 * field - 4.0 * back_one + back_two)
    minus = -0.5 * (3.0 * field - 4.0 * fore_one + fore_two)
    return speed * jnp.where(speed > 0, plus, minus)


def transport(state, vx, vy):
    cols = state.shape[1]
    padded = with_halo(state, (("space", 1),), 2)
    centre = padded[:, 2 : cols + 2]
    plus = 0.5 * (3.0 * centre - 4.0 * padded[:, 1 : cols + 1] + padded[:, 0:cols])
    minus = -0.5 * (3.0 * centre - 4.0 * padded[:, 3 : cols + 3] + padded[:, 4 : cols + 4])
    speed = vx[:, None, None]
    across = speed * jnp.where(speed > 0, plus, minus)
    return centre - step_ratio * (across + upwind_y(centre, vy[:, None, None]))


def shards(distribution, wall_mask):
    vel_count = lax.axis_size("vel")
    rank = lax.axis_index("vel")
    block = distribution.shape[0]
    cols = distribution.shape[1]
    vx, vy, vz = velocity_nodes(rank * block, block, NODES)
    table = moment_table(vx, vy, vz, NODES)
    has_wall = jnp.max(wall_mask, axis=1)
    layer_ids = jnp.arange(cols, dtype=jnp.int32)
    first_wall = jnp.min(jnp.where(has_wall > 0, layer_ids, cols))
    start = jnp.minimum(first_wall, cols - 2)
    wall_slab = lax.dynamic_slice_in_dim(wall_mask, start, 2, 0) > 0
    state = distribution
    for step in range(STEPS):
        moved = transport(state, vx, vy)
        slab = lax.dynamic_slice_in_dim(moved, start, 2, 1)
        partner = slab
        for bit in range(vel_count.bit_length() - 1):
            partner = swapped(partner, "vel", bit)
        flipped = partner[::-1]
        new_slab = jnp.where(wall_slab[None], flipped, slab)
        reflected = lax.dynamic_update_slice_in_dim(moved, new_slab, start, 1)
        partial_value = jnp.dot(
            table,
            reflected.reshape(block, -1),
            precision=lax.Precision.HIGHEST,
            preferred_element_type=jnp.float32,
        )
        params = shakhov_params(lax.psum(partial_value, "vel"))
        state = relax(reflected, params, vx, vy, vz)
    return state


def solution(mesh):
    placed = (P("vel", "space", None), P("space", None))
    return jax.shard_map(
        shards, mesh=mesh, in_specs=placed, out_specs=P("vel", "space", None), check_vma=False
    )
```

profile of v0, /device:TPU:40, one launch (start us, length us, event | category | flops | bytes accessed | tf_op | source)
XLA Modules:
  0.0 467.0 jit_solution(10270056307525062764)
XLA Ops:
  0.0 2.9 fusion.134
  3.9 1.9 collective-permute-start
  22.5 21.5 %collective-permute-done = f32[864,2,128]{2,0,1:T(8,128)} collective-permute-done((f32[864,2,128]{2,0,1:T(8,128)}, f32[864,2,128]{2,0,1:T(8,128)}, u32[]{:S(2)}, u32[]{:S(2)}) %collective-permute-start) | collective-permute-done | bytes 884768 | tf_op jit(solution)/shard_map/ppermute | solution.py:28
  48.5 5.1 %fusion.62 = f32[864,4,128]{2,0,1:T(8,128)S(1)} fusion(f32[864,6,128]{2,0,1:T(8,128)S(1)} %constant_dynamic-update-slice_fusion.2, f32[864,6,128]{2,0,1:T(8,128)S(1)} %get-tuple-element.37, f32[864,4,127]{2,0,1:T(8,128)S(1)} %copy-done.1, f32[864,4,1]{2,0,1:T(8,128)S(1)} %copy-done.2, f32[864,4,126]{2,0,1:T(8,128)S(1)} %copy-done.3, ...), kind=kLoop, calls=%fused_computation.83 | loop fusion | flops 12386304 | bytes 17703360 | tf_op jit(solution)/shard_map/sub | solution.py:147
  53.8 2.4 collective-permute-done.2
  56.2 3.1 collective-permute-start.3
  59.3 23.5 %collective-permute-done.3 = f32[864,2,128]{2,0,1:T(8,128)S(1)} collective-permute-done((f32[864,2,128]{2,0,1:T(8,128)S(1)}, f32[864,2,128]{2,0,1:T(8,128)S(1)}, u32[]{:S(2)}, u32[]{:S(2)}) %collective-permute-start.3) | collective-permute-done | bytes 884768 | tf_op jit(solution)/shard_map/ppermute | solution.py:44
  84.3 19.3 %collective-permute-done.4 = f32[864,2,128]{2,0,1:T(8,128)} collective-permute-done((f32[864,2,128]{2,0,1:T(8,128)S(1)}, f32[864,2,128]{2,0,1:T(8,128)}, u32[]{:S(2)}, u32[]{:S(2)}) %collective-permute-start.4) | collective-permute-done | bytes 884768 | tf_op jit(solution)/shard_map/ppermute | solution.py:44
  103.6 3.0 collective-permute-start.5
  109.0 16.0 %collective-permute-done.5 = f32[864,2,128]{2,0,1:T(8,128)S(1)} collective-permute-done((f32[864,2,128]{2,0,1:T(8,128)}, f32[864,2,128]{2,0,1:T(8,128)S(1)}, u32[]{:S(2)}, u32[]{:S(2)}) %collective-permute-start.5) | collective-permute-done | bytes 884768 | tf_op jit(solution)/shard_map/ppermute | solution.py:44
  128.5 3.1 fusion.74
  131.6 86.7 %psum.14 = f32[13,512]{1,0:T(8,128)S(1)} all-reduce(f32[13,512]{1,0:T(8,128)S(1)} %fusion.74), channel_id=1, replica_groups=mesh['space'=16,'vel'=16] {'vel'}, use_global_device_ids=true, to_apply=%region_2.3 | all-reduce | flops 6656 | bytes 53248 | tf_op jit(solution)/shard_map/psum | solution.py:178
  221.2 2.9 collective-permute-start.7
  224.1 19.7 %collective-permute-start.6 = (f32[864,2,128]{2,0,1:T(8,128)S(1)}, f32[864,2,128]{2,0,1:T(8,128)S(1)}, u32[]{:S(2)}, u32[]{:S(2)}) collective-permute-start(f32[864,2,128]{2,0,1:T(8,128)S(1)} %get-tuple-element.27), channel_id=1, source_target_pairs={{0,16},{16,32},{32,48},{48,64},{64,80},{80,96},{96,112},{112,128},... | collective-permute-start | bytes 2654216 | tf_op jit(solution)/shard_map/ppermute | solution.py:28
  245.5 17.9 %collective-permute-done.7 = f32[864,2,128]{2,0,1:T(8,128)S(1)} collective-permute-done((f32[864,2,128]{2,0,1:T(8,128)S(1)}, f32[864,2,128]{2,0,1:T(8,128)S(1)}, u32[]{:S(2)}, u32[]{:S(2)}) %collective-permute-start.7) | collective-permute-done | bytes 884768 | tf_op jit(solution)/shard_map/ppermute | solution.py:30
  263.3 12.7 %collective-permute-done.6 = f32[864,2,128]{2,0,1:T(8,128)S(1)} collective-permute-done((f32[864,2,128]{2,0,1:T(8,128)S(1)}, f32[864,2,128]{2,0,1:T(8,128)S(1)}, u32[]{:S(2)}, u32[]{:S(2)}) %collective-permute-start.6) | collective-permute-done | bytes 884768 | tf_op jit(solution)/shard_map/ppermute | solution.py:28
  276.0 3.3 fusion.45
  279.5 2.4 collective-permute-done.8
  281.9 44.4 %collective-permute-done.9 = f32[864,2,128]{2,0,1:T(8,128)S(1)} collective-permute-done((f32[864,2,128]{2,0,1:T(8,128)S(1)}, f32[864,2,128]{2,0,1:T(8,128)S(1)}, u32[]{:S(2)}, u32[]{:S(2)}) %collective-permute-start.9) | collective-permute-done | bytes 884768 | tf_op jit(solution)/shard_map/ppermute | solution.py:44
  326.3 20.9 %collective-permute-done.10 = f32[864,2,128]{2,0,1:T(8,128)S(1)} collective-permute-done((f32[864,2,128]{2,0,1:T(8,128)S(1)}, f32[864,2,128]{2,0,1:T(8,128)S(1)}, u32[]{:S(2)}, u32[]{:S(2)}) %collective-permute-start.10) | collective-permute-done | bytes 884768 | tf_op jit(solution)/shard_map/ppermute | solution.py:44
  348.6 20.1 %collective-permute-done.11 = f32[864,2,128]{2,0,1:T(8,128)S(1)} collective-permute-done((f32[864,2,128]{2,0,1:T(8,128)S(1)}, f32[864,2,128]{2,0,1:T(8,128)S(1)}, u32[]{:S(2)}, u32[]{:S(2)}) %collective-permute-start.11) | collective-permute-done | bytes 884768 | tf_op jit(solution)/shard_map/ppermute | solution.py:44
  371.6 3.1 fusion.72
  374.7 87.8 %psum.15 = f32[13,512]{1,0:T(8,128)S(1)} all-reduce(f32[13,512]{1,0:T(8,128)S(1)} %fusion.72), channel_id=1, replica_groups=mesh['space'=16,'vel'=16] {'vel'}, use_global_device_ids=true, to_apply=%region_3.4 | all-reduce | flops 6656 | bytes 53248 | tf_op jit(solution)/shard_map/psum | solution.py:178
  464.6 2.3 copy.34
  (92 shorter events, 39.9 us)
Async XLA Ops:
  2.9 3.2 copy-start
  3.9 40.1 %collective-permute-start = (f32[864,2,128]{2,0,1:T(8,128)}, f32[864,2,128]{2,0,1:T(8,128)}, u32[]{:S(2)}, u32[]{:S(2)}) collective-permute-start(f32[864,2,128]{2,0,1:T(8,128)} %copy.39), channel_id=1, source_target_pairs={{0,16},{16,32},{32,48},{48,64},{64,80},{80,96},{96,112},{112,128},... | collective-permute-start | bytes 2654216 | tf_op jit(solution)/shard_map/ppermute | solution.py:28
  5.9 40.1 %collective-permute-start.1 = (f32[864,2,128]{2,0,1:T(8,128)S(1)}, f32[864,2,128]{2,0,1:T(8,128)S(1)}, u32[]{:S(2)}, u32[]{:S(2)}) collective-permute-start(f32[864,2,128]{2,0,1:T(8,128)S(1)} %copy.38), channel_id=1, source_target_pairs={{16,0},{32,16},{48,32},{64,48},{80,64},{96,80},{112,96},{128,112},... | collective-permute-start | bytes 2654216 | tf_op jit(solution)/shard_map/ppermute | solution.py:30
  22.5 23.6 %copy-start.8 = (pred[864]{0:T(1024)(128)(4,1)}, pred[864]{0:T(1024)(128)(4,1)S(1)}, u32[]{:S(2)}) copy-start(pred[864]{0:T(1024)(128)(4,1)S(1)} %get-tuple-element.62) | copy-start | bytes 2596
  44.0 2.0 copy-start.5
  45.4 1.6 copy-start.2
  45.4 2.1 copy-start.3
  45.4 2.6 copy-start.4
  45.7 2.8 copy-start.1
  53.6 54.8 %copy-start.12 = (s32[4,128]{1,0:T(4,128)S(1)}, s32[4,128]{1,0:T(4,128)}, u32[]{:S(2)}) copy-start(s32[4,128]{1,0:T(4,128)} %param.3) | copy-start | bytes 6148
  53.7 2.5 collective-permute-start.2
  56.2 26.6 %collective-permute-start.3 = (f32[864,2,128]{2,0,1:T(8,128)S(1)}, f32[864,2,128]{2,0,1:T(8,128)S(1)}, u32[]{:S(2)}, u32[]{:S(2)}) collective-permute-start(f32[864,2,128]{2,0,1:T(8,128)S(1)} %collective-permute-done.2), channel_id=1, source_target_pairs={{0,2},{2,0},{1,3},{3,1},{4,6},{6,4},{5,7},{7,5},{8,10},{10,8},{9,1... | collective-permute-start | bytes 2654216 | tf_op jit(solution)/shard_map/ppermute | solution.py:44
  82.8 20.7 %collective-permute-start.4 = (f32[864,2,128]{2,0,1:T(8,128)S(1)}, f32[864,2,128]{2,0,1:T(8,128)}, u32[]{:S(2)}, u32[]{:S(2)}) collective-permute-start(f32[864,2,128]{2,0,1:T(8,128)S(1)} %collective-permute-done.3), channel_id=1, source_target_pairs={{0,4},{4,0},{1,5},{5,1},{2,6},{6,2},{3,7},{7,3},{8,12},{12,8},{9,1... | collective-permute-start | bytes 2654216 | tf_op jit(solution)/shard_map/ppermute | solution.py:44
  103.6 21.4 %collective-permute-start.5 = (f32[864,2,128]{2,0,1:T(8,128)}, f32[864,2,128]{2,0,1:T(8,128)S(1)}, u32[]{:S(2)}, u32[]{:S(2)}) collective-permute-start(f32[864,2,128]{2,0,1:T(8,128)} %collective-permute-done.4), channel_id=1, source_target_pairs={{0,8},{8,0},{1,9},{9,1},{2,10},{10,2},{3,11},{11,3},{4,12},{12,4},... | collective-permute-start | bytes 2654216 | tf_op jit(solution)/shard_map/ppermute | solution.py:44
  126.8 1.7 copy-start.6
  221.2 42.2 %collective-permute-start.7 = (f32[864,2,128]{2,0,1:T(8,128)S(1)}, f32[864,2,128]{2,0,1:T(8,128)S(1)}, u32[]{:S(2)}, u32[]{:S(2)}) collective-permute-start(f32[864,2,128]{2,0,1:T(8,128)S(1)} %get-tuple-element.28), channel_id=1, source_target_pairs={{16,0},{32,16},{48,32},{64,48},{80,64},{96,80},{112,96},{128,112},... | collective-permute-start | bytes 2654216 | tf_op jit(solution)/shard_map/ppermute | solution.py:30
  224.1 51.9 %collective-permute-start.6 = (f32[864,2,128]{2,0,1:T(8,128)S(1)}, f32[864,2,128]{2,0,1:T(8,128)S(1)}, u32[]{:S(2)}, u32[]{:S(2)}) collective-permute-start(f32[864,2,128]{2,0,1:T(8,128)S(1)} %get-tuple-element.27), channel_id=1, source_target_pairs={{0,16},{16,32},{32,48},{48,64},{64,80},{80,96},{96,112},{112,128},... | collective-permute-start | bytes 2654216 | tf_op jit(solution)/shard_map/ppermute | solution.py:28
  244.9 31.1 %copy-start.9 = (pred[864]{0:T(1024)(128)(4,1)S(1)}, pred[864]{0:T(1024)(128)(4,1)}, u32[]{:S(2)}) copy-start(pred[864]{0:T(1024)(128)(4,1)} %copy-done.8) | copy-start | bytes 2596
  279.3 90.4 %copy-start.10 = (pred[2,128]{1,0:T(4,128)(4,1)S(1)}, pred[2,128]{1,0:T(4,128)(4,1)}, u32[]{:S(2)}) copy-start(pred[2,128]{1,0:T(4,128)(4,1)} %fusion.112) | copy-start | bytes 772
  279.4 2.5 collective-permute-start.8
  281.9 44.4 %collective-permute-start.9 = (f32[864,2,128]{2,0,1:T(8,128)S(1)}, f32[864,2,128]{2,0,1:T(8,128)S(1)}, u32[]{:S(2)}, u32[]{:S(2)}) collective-permute-start(f32[864,2,128]{2,0,1:T(8,128)S(1)} %collective-permute-done.8), channel_id=1, source_target_pairs={{0,2},{2,0},{1,3},{3,1},{4,6},{6,4},{5,7},{7,5},{8,10},{10,8},{9,1... | collective-permute-start | bytes 2654216 | tf_op jit(solution)/shard_map/ppermute | solution.py:44
  326.3 20.9 %collective-permute-start.10 = (f32[864,2,128]{2,0,1:T(8,128)S(1)}, f32[864,2,128]{2,0,1:T(8,128)S(1)}, u32[]{:S(2)}, u32[]{:S(2)}) collective-permute-start(f32[864,2,128]{2,0,1:T(8,128)S(1)} %collective-permute-done.9), channel_id=1, source_target_pairs={{0,4},{4,0},{1,5},{5,1},{2,6},{6,2},{3,7},{7,3},{8,12},{12,8},{9,1... | collective-permute-start | bytes 2654216 | tf_op jit(solution)/shard_map/ppermute | solution.py:44
  347.2 21.5 %collective-permute-start.11 = (f32[864,2,128]{2,0,1:T(8,128)S(1)}, f32[864,2,128]{2,0,1:T(8,128)S(1)}, u32[]{:S(2)}, u32[]{:S(2)}) collective-permute-start(f32[864,2,128]{2,0,1:T(8,128)S(1)} %collective-permute-done.10), channel_id=1, source_target_pairs={{0,8},{8,0},{1,9},{9,1},{2,10},{10,2},{3,11},{11,3},{4,12},{12,4},... | collective-permute-start | bytes 2654216 | tf_op jit(solution)/shard_map/ppermute | solution.py:44
  369.9 1.7 copy-start.7
  (1 other events, 1.3 us)
where the time goes:
time: 467 us
  waiting for transfers between devices  201 us (43%)
  blocking collectives  175 us (37%)
  local copies, waits for them, and re-layouts  34.4 us (7%)
  starting transfers between devices  33.9 us (7%)
  other arithmetic  15.5 us (3%)
  matrix products  6.19 us (1%)
    psum x2, blocking collectives, shards(): params = shakhov_params(lax.psum(partial_value, 'vel'))  175 us
    ppermute x8, waiting for transfers between devices, swapped(): return lax.ppermute(block, axis, route)  149 us
    ppermute x2, waiting for transfers between devices, with_halo(): lax.ppermute(tail, axis, [(i, (i + 1) % count) for i in range(count)])  34.2 us
    ppermute x2, starting transfers between devices, with_halo(): lax.ppermute(tail, axis, [(i, (i + 1) % count) for i in range(count)])  21.6 us
    ppermute x2, waiting for transfers between devices, with_halo(): lax.ppermute(head, axis, [((i + 1) % count, i) for i in range(count)])  18.2 us
    unnamed x37, local copies, waits for them, and re-layouts  15.7 us
  transfers between devices with their start and end apart: 12, of which 12 were waited for; matrix products, arithmetic and copies ran while one was open for 5% of the time, Pallas kernels for 0%

commit v1 on v0

v1 whole, which is shorter than its diff:
```python
import functools
import math

import jax
import jax.numpy as jnp
from jax import lax
from jax.experimental import pallas as pl
from jax.experimental.pallas import tpu as pltpu
from jax.sharding import PartitionSpec as P

MESH = pl.DeviceIdType.MESH
SPACE = 16
VEL = 16
ROWS = 864
COLS = 4
LANES = 128
CHUNKS = 6
CROWS = ROWS // CHUNKS
NODE = 9.0 / 24.0
WEIGHT = NODE**3 / (2.0 * math.pi) ** 1.5
STEP = 0.1
F32 = jnp.float32


def signal(sem, device):
    pl.semaphore_signal(sem, inc=1, device_id=device, device_id_type=MESH)


def remote(src, dst, send, recv, device):
    return pltpu.make_async_remote_copy(
        src_ref=src, dst_ref=dst, send_sem=send, recv_sem=recv, device_id=device, device_id_type=MESH
    )


class Place:
    def __init__(self):
        self.s = lax.axis_index("space")
        self.v = lax.axis_index("vel")
        self.pos = self.v // 8
        ahead = self.pos * 2 - 1
        self.down = (lax.rem(self.s + ahead + SPACE, SPACE), self.v)
        self.up = (lax.rem(self.s - ahead + SPACE, SPACE), self.v)
        self.block = jnp.where(self.pos == 1, 15 - self.v, self.v)
        self.core = lax.rem(self.v, 2)
        self.chip = self.v // 2

    def layer(self, flow):
        return self.pos * (2 * flow - 3) + 3 - flow

    def group(self, g):
        index = 3 * self.block + jnp.where(self.pos == 1, 2 - g, g)
        half = lax.rem(index, 2)
        speed = 4.5 - ((index // 2).astype(F32) + 0.5) * NODE
        first = 12 * half + jnp.where(self.pos == 1, 11, 0)
        slope = (1 - 2 * self.pos).astype(F32) * NODE
        y0 = (first.astype(F32) + 0.5) * NODE - 4.5
        return speed, half, y0, slope

    def vx(self, speed):
        return speed * (2 * self.pos - 1).astype(F32)

    def z(self, t):
        sub = lax.broadcasted_iota(jnp.int32, (8, LANES), 0).astype(F32)
        return ((sub + (8 * t + 0.5)) * NODE - 4.5) * (1 - 2 * self.pos).astype(F32)


def at(row):
    return pl.ds(pl.multiple_of(row, 8), 8)


def transport(place, field, moved, flows, g, first, count):
    speed, half, y0, slope = place.group(g)
    shift = jnp.where(half == 1, 1, LANES - 1)
    alpha = STEP * speed

    def run(r, carry):
        beta = STEP * jnp.abs(y0 + slope * r.astype(F32))
        keep = 1.0 - 1.5 * (alpha + beta)
        for t in range(3):
            rows = at((g * 12 + r) * 24 + 8 * t)
            lines = {l: field[l, rows, :] for l in range(flows[0], flows[-1] + 3)}
            for l in flows:
                own = lines[l + 2]
                near = own - 0.25 * pltpu.roll(own, shift, 1)
                near = pltpu.roll(near, shift, 1)
                moved[l, rows, :] = (
                    keep * own
                    + (2.0 * alpha) * (lines[l + 1] - 0.25 * lines[l])
                    + (2.0 * beta) * near
                )
        return carry

    lax.fori_loop(first, first + count, run, 0)


def moments(place, field, part, sums, z_sums):
    def group(g, carry):
        speed, half, y0, slope = place.group(g)
        x = place.vx(speed)
        for t in range(3):

            def run(r, acc):
                y = y0 + slope * r.astype(F32)
                rows = at((g * 12 + r) * 24 + 8 * t)
                out = []
                for l in range(COLS):
                    f0 = field[l, rows, :]
                    f1 = y * f0
                    f2 = y * f1
                    f3 = y * f2
                    out += [acc[4 * l] + f0, acc[4 * l + 1] + f1, acc[4 * l + 2] + f2, acc[4 * l + 3] + f3]
                return tuple(out)

            acc = lax.fori_loop(0, 12, run, (jnp.zeros((8, LANES), F32),) * 16)
            z = place.z(t)
            for l in range(COLS):
                a, b, c, d = acc[4 * l : 4 * l + 4]
                za = z * a
                zb = z * b
                zza = z * za
                terms = [a, b, c, d, za, zb, z * c, zza, z * zb, z * zza]
                for m, term in enumerate(terms):
                    if t == 0:
                        z_sums[l, m] = term
                    else:
                        z_sums[l, m] = z_sums[l, m] + term
        for l in range(COLS):
            a, b, c, d, za, zb, zc, zza, zzb, zzza = [z_sums[l, m] for m in range(10)]
            xx = x * x
            rows13 = [
                a,
                x * a,
                b,
                za,
                xx * a,
                c,
                zza,
                x * b,
                x * za,
                zb,
                x * (xx * a + c + zza),
                xx * b + d + zzb,
                xx * za + zc + zzza,
            ]
            for m, value in enumerate(rows13):
                part[l, m] = part[l, m] + value
        return carry

    part[...] = jnp.zeros_like(part)
    lax.fori_loop(0, 3, group, 0)
    for l in range(COLS):
        rows = [jnp.sum(part[l, m], axis=0, keepdims=True) * WEIGHT for m in range(13)]
        sums[place.layer(l)] = jnp.concatenate(rows + [jnp.zeros((3, LANES), F32)], axis=0)


def cell_params(m):
    raw = m[0]
    density = jnp.maximum(raw, 0.1)
    mx, my, mz = m[1], m[2], m[3]
    inv = 1.0 / density
    ux, uy, uz = mx * inv, my * inv, mz * inv
    sxx, syy, szz, sxy, sxz, syz = m[4:10]
    energy = sxx + syy + szz
    speed2 = ux * ux + uy * uy + uz * uz
    temper = jnp.maximum((energy * inv - speed2) / 3.0, 0.1)
    along = ux * mx + uy * my + uz * mz

    def heat(third, first, uval, dot_row):
        return 0.5 * (
            third
            - 2.0 * dot_row
            + speed2 * first
            - uval * energy
            + 2.0 * uval * along
            - uval * speed2 * raw
        )

    qx = heat(m[10], mx, ux, ux * sxx + uy * sxy + uz * sxz)
    qy = heat(m[11], my, uy, ux * sxy + uy * syy + uz * syz)
    qz = heat(m[12], mz, uz, ux * sxz + uy * syz + uz * szz)
    factor = (STEP / 0.5) * density * jnp.exp(0.19 * jnp.log(temper))
    inv_t = 1.0 / temper
    scale = (1.0 - 2.0 / 3.0) / (5.0 * density * temper * temper)
    peak = density * inv_t * lax.rsqrt(temper)
    return [ux, uy, uz, 0.5 * inv_t, inv_t, peak * factor, scale * qx, scale * qy, scale * qz, 1.0 - factor]


def spread(row):
    return jnp.broadcast_to(row, (8, LANES))


def relax(place, load, store, params, p, table):
    ux, uy, uz, half_t, inv_t, peak, kx, ky, kz, keep = [params[p, pl.ds(i, 1), :] for i in range(10)]
    z_exp, z_dot, z_square = [], [], []
    for t in range(3):
        c = place.z(t) - spread(uz)
        z_exp.append(jnp.exp(-(c * c) * spread(half_t)))
        z_dot.append(c * spread(kz))
        z_square.append(c * c * spread(inv_t))
    keep8 = spread(keep)
    for g in range(3):
        speed, half, y0, slope = place.group(g)
        cx = place.vx(speed) - ux
        for part in range(2):
            index = lax.broadcasted_iota(jnp.int32, (8, LANES), 0).astype(F32) + 8.0 * part
            cy = (y0 + slope * index) - spread(uy)
            square = spread(cx * cx) + cy * cy
            rows = pl.ds(16 * g + 8 * part, 8)
            table[0, rows, :] = spread(peak) * jnp.exp(-square * spread(half_t))
            table[1, rows, :] = spread(cx * kx) + cy * spread(ky)
            table[2, rows, :] = square * spread(inv_t) - 5.0
    for g in range(3):

        def run(r, carry):
            line = pl.ds(16 * g + r, 1)
            amp = spread(table[0, line, :])
            dot = spread(table[1, line, :])
            square = spread(table[2, line, :])
            for t in range(3):
                row = (g * 12 + r) * 24 + 8 * t
                old = load(row)
                shape = 1.0 + (dot + z_dot[t]) * (square + z_square[t])
                store(row, keep8 * old + (amp * z_exp[t]) * shape)
            return carry

        lax.fori_loop(0, 12, run, 0, unroll=2)


def flip8(x):
    sub = lax.broadcasted_iota(jnp.int32, (8, LANES), 0)
    x = pltpu.roll(x, 4, 0)
    x = jnp.where(sub % 4 < 2, pltpu.roll(x, 6, 0), pltpu.roll(x, 2, 0))
    return jnp.where(sub % 2 < 1, pltpu.roll(x, 7, 0), pltpu.roll(x, 1, 0))


def first_kernel(x_ref, mask_ref, moved, walls, where, raw, field, note, hear, in_sem, ssem, rsem, nsem, hsem):
    place = Place()
    s, v = place.s, place.v
    span = CROWS * COLS
    loads = [
        pltpu.make_async_copy(x_ref.at[pl.ds(c * span, span)], raw.at[pl.ds(c * span, span)], in_sem.at[c])
        for c in range(CHUNKS)
    ]
    for copy in loads:
        copy.start()

    line, z = s // 4, lax.rem(s, 4)
    mates = [(line * 4 + lax.rem(z + i, 4), v) for i in range(1, 4)]
    cross = [(lax.rem(line + i, 4) * 4 + z, v) for i in range(1, 4)]
    barrier = pltpu.get_barrier_semaphore()
    for device in [place.up] + mates + cross:
        signal(barrier, device)

    mask = mask_ref[...].astype(F32)
    has = [jnp.broadcast_to(jnp.max(mask[i : i + 1, :], axis=1, keepdims=True), (1, LANES)) for i in range(COLS)]
    first = has[0]
    second = (1.0 - has[0]) * has[1]
    walls[0:4, :] = mask
    walls[4:8, :] = jnp.concatenate([first, second, 1.0 - first - second, jnp.zeros_like(first)], axis=0)
    here = jnp.maximum(jnp.maximum(has[1], has[2]), has[3]) * s.astype(F32)
    note[0] = spread(here)

    def split(flows, c):
        def body(i, carry):
            row = c * CROWS + 8 * i
            for l in flows:
                field[l + 2, at(row), :] = raw[pl.ds(row * COLS + place.layer(l), 8, stride=COLS), :]
            return carry

        lax.fori_loop(0, CROWS // 8, body, 0, unroll=2)

    sends = []
    for c in range(CHUNKS):
        loads[c].wait()
        split((2, 3), c)
        if c == 0:
            pl.semaphore_wait(barrier, 7)
        rows = pl.ds(c * CROWS, CROWS)
        copy = remote(
            field.at[pl.ds(4, 2), rows], field.at[pl.ds(0, 2), rows], ssem.at[c], rsem.at[c], place.down
        )
        copy.start()
        sends.append(copy)
    words = [remote(note.at[0], hear.at[i], nsem.at[i], hsem.at[i], mates[i]) for i in range(3)]
    for copy in words:
        copy.start()
    for c in range(CHUNKS):
        split((0, 1), c)
    for copy in words:
        copy.wait_recv()
    note[1] = note[0] + hear[0] + hear[1] + hear[2]
    more = [remote(note.at[1], hear.at[3 + i], nsem.at[3 + i], hsem.at[3 + i], cross[i]) for i in range(3)]
    for copy in more:
        copy.start()

    def later(g, carry):
        transport(place, field, moved, (2, 3), g, 0, 12)
        return carry

    lax.fori_loop(0, 3, later, 0)
    for copy in more:
        copy.wait_recv()
    total = note[1] + hear[3] + hear[4] + hear[5]
    where[0] = jnp.max(total).astype(jnp.int32)
    for c in range(CHUNKS):
        sends[c].wait_recv()
        transport(place, field, moved, (0, 1), c // 2, 6 * (c % 2), 6)
    for copy in sends + words + more:
        copy.wait_send()


def second_kernel(
    block,
    moved_ref,
    walls,
    out,
    one,
    halo,
    field,
    two,
    slab,
    mirror,
    part,
    z_sums,
    sums,
    swap,
    gather,
    params,
    edge,
    table,
    in_sem,
    hsem,
    xsem,
    psem,
    esem,
):
    place = Place()
    s, v = place.s, place.v
    load = pltpu.make_async_copy(moved_ref, one, in_sem)
    load.start()
    after = (block + 1) % SPACE
    near_wall = jnp.logical_or(s == block, s == after)
    partner = (s, 15 - v)
    peer = (s, v + 1 - 2 * place.core)
    chips = [lax.rem(place.chip + i, 8) for i in range(1, 8)]
    mates = [(s, 2 * chip + place.core) for chip in chips]

    barrier = pltpu.get_barrier_semaphore()
    for device in [place.up, peer] + mates:
        signal(barrier, device)

    @pl.when(near_wall)
    def _():
        signal(barrier, partner)
        pl.semaphore_wait(barrier, 10)

    @pl.when(jnp.logical_not(near_wall))
    def _():
        pl.semaphore_wait(barrier, 9)

    load.wait()

    def reflect(state, k):
        def cut(i, carry):
            rows = at(8 * i)
            lines = [state[place.layer(l), rows, :] for l in range(COLS)]
            at0 = spread(walls[4:5, :]) > 0.5
            at1 = spread(walls[5:6, :]) > 0.5
            slab[k, 0, rows, :] = jnp.where(at0, lines[0], jnp.where(at1, lines[1], lines[2]))
            slab[k, 1, rows, :] = jnp.where(at0, lines[1], jnp.where(at1, lines[2], lines[3]))
            return carry

        def put(i, carry):
            rows = at(8 * i)
            back = at(ROWS - 8 - 8 * i)
            near = flip8(mirror[k, 0, back, :])
            far = flip8(mirror[k, 1, back, :])
            for l in range(COLS):
                new = jnp.where(spread(walls[4 + l : 5 + l, :]) > 0.5, near, far)
                line = place.layer(l)
                state[line, rows, :] = jnp.where(spread(walls[l : l + 1, :]) > 0.5, new, state[line, rows, :])
            return carry

        @pl.when(s == block)
        def _():
            lax.fori_loop(0, ROWS // 8, cut, 0)
            copy = remote(slab.at[k], mirror.at[k], xsem.at[k, 0], xsem.at[k, 1], partner)
            copy.start()
            copy.wait()
            lax.fori_loop(0, ROWS // 8, put, 0)

        @pl.when(s == after)
        def _():
            lax.fori_loop(0, ROWS // 8, cut, 0)
            mirror[k, 1] = jnp.zeros((ROWS, LANES), F32)
            copy = remote(slab.at[k, 0], mirror.at[k, 0], xsem.at[k, 0], xsem.at[k, 1], partner)
            copy.start()
            copy.wait()
            lax.fori_loop(0, ROWS // 8, put, 0)

    def total(k):
        mine = pl.ds(2 * place.core, 2)
        first = remote(
            sums.at[k, pl.ds(2 - 2 * place.core, 2)], swap.at[k], psem.at[k, 0, 0], psem.at[k, 1, 0], peer
        )
        first.start()
        first.wait_recv()
        gather[k, place.chip] = sums[k, mine] + swap[k]
        outs = []
        for i, mate in enumerate(mates):
            copy = remote(
                gather.at[k, place.chip], gather.at[k, place.chip], psem.at[k, 0, i + 1], psem.at[k, 1, i + 1], mate
            )
            copy.start()
            outs.append(copy)
        for copy in outs:
            copy.wait_recv()
        whole = gather[k, 0]
        for i in range(1, 8):
            whole = whole + gather[k, i]
        rows = cell_params([whole[:, i, :] for i in range(13)])
        for i, row in enumerate(rows):
            params[k, mine, i, :] = row
        last = remote(params.at[k, mine], params.at[k, mine], psem.at[k, 0, 8], psem.at[k, 1, 8], peer)
        last.start()
        last.wait_recv()
        return [first, last] + outs

    reflect(one, 0)
    hand = remote(one.at[pl.ds(2, 2)], halo, hsem.at[0], hsem.at[1], place.down)
    hand.start()
    moments(place, one, part, sums.at[0], z_sums)
    open_copies = total(0)
    tell = remote(
        params.at[0, pl.ds(2 * place.pos, 2)], edge, esem.at[0], esem.at[1], place.down
    )
    tell.start()

    def own(l, carry):
        def load_row(row):
            return one[l, at(row), :]

        def store_row(row, value):
            field[l + 2, at(row), :] = value

        relax(place, load_row, store_row, params.at[0], place.layer(l), table)
        return carry

    lax.fori_loop(0, COLS, own, 0)
    tell.wait_recv()
    hand.wait_recv()

    def beside(l, carry):
        def load_row(row):
            return halo[l, at(row), :]

        def store_row(row, value):
            field[l, at(row), :] = value

        relax(place, load_row, store_row, edge, jnp.where(place.pos == 1, l, 1 - l), table)
        return carry

    lax.fori_loop(0, 2, beside, 0)

    def step(g, carry):
        transport(place, field, two, (0, 1, 2, 3), g, 0, 12)
        return carry

    lax.fori_loop(0, 3, step, 0)

    reflect(two, 1)
    moments(place, two, part, sums.at[1], z_sums)
    open_copies += total(1)

    def end(l, carry):
        layer = place.layer(l)

        def load_row(row):
            return two[l, at(row), :]

        def store_row(row, value):
            out[pl.ds(row * COLS + layer, 8, stride=COLS), :] = value

        relax(place, load_row, store_row, params.at[1], layer, table)
        return carry

    lax.fori_loop(0, COLS, end, 0)
    for copy in open_copies + [hand, tell]:
        copy.wait_send()


def first_call(x, mask):
    dma = pltpu.SemaphoreType.DMA
    return pl.pallas_call(
        first_kernel,
        out_shape=(
            jax.ShapeDtypeStruct((COLS, ROWS, LANES), F32),
            jax.ShapeDtypeStruct((8, LANES), F32),
            jax.ShapeDtypeStruct((1,), jnp.int32),
        ),
        in_specs=[pl.BlockSpec(memory_space=pl.ANY), pl.BlockSpec(memory_space=pltpu.VMEM)],
        out_specs=(
            pl.BlockSpec(memory_space=pltpu.VMEM),
            pl.BlockSpec(memory_space=pltpu.VMEM),
            pl.BlockSpec(memory_space=pltpu.SMEM),
        ),
        scratch_shapes=[
            pltpu.VMEM((ROWS * COLS, LANES), F32),
            pltpu.VMEM((COLS + 2, ROWS, LANES), F32),
            pltpu.VMEM((2, 8, LANES), F32),
            pltpu.VMEM((6, 8, LANES), F32),
            dma((CHUNKS,)),
            dma((CHUNKS,)),
            dma((CHUNKS,)),
            dma((6,)),
            dma((6,)),
        ],
        compiler_params=pltpu.CompilerParams(
            collective_id=0, has_side_effects=True, vmem_limit_bytes=24 << 20
        ),
        name="first",
    )(x, mask)


def second_call(block, moved, walls):
    dma = pltpu.SemaphoreType.DMA
    return pl.pallas_call(
        functools.partial(second_kernel, block),
        out_shape=jax.ShapeDtypeStruct((ROWS * COLS, LANES), F32),
        in_specs=[pl.BlockSpec(memory_space=pl.ANY), pl.BlockSpec(memory_space=pltpu.VMEM)],
        out_specs=pl.BlockSpec(memory_space=pltpu.VMEM),
        scratch_shapes=[
            pltpu.VMEM((COLS, ROWS, LANES), F32),
            pltpu.VMEM((2, ROWS, LANES), F32),
            pltpu.VMEM((COLS + 2, ROWS, LANES), F32),
            pltpu.VMEM((COLS, ROWS, LANES), F32),
            pltpu.VMEM((2, 2, ROWS, LANES), F32),
            pltpu.VMEM((2, 2, ROWS, LANES), F32),
            pltpu.VMEM((COLS, 13, 8, LANES), F32),
            pltpu.VMEM((COLS, 10, 8, LANES), F32),
            pltpu.VMEM((2, COLS, 16, LANES), F32),
            pltpu.VMEM((2, 2, 16, LANES), F32),
            pltpu.VMEM((2, 8, 2, 16, LANES), F32),
            pltpu.VMEM((2, COLS, 16, LANES), F32),
            pltpu.VMEM((2, 16, LANES), F32),
            pltpu.VMEM((3, 48, LANES), F32),
            dma,
            dma((2,)),
            dma((2, 2)),
            dma((2, 2, 9)),
            dma((2,)),
        ],
        compiler_params=pltpu.CompilerParams(
            collective_id=1 + block, has_side_effects=True, vmem_limit_bytes=32 << 20
        ),
        name=f"second{block}",
    )(moved, walls)


def shards(distribution, wall_mask):
    x = distribution.reshape(ROWS * COLS, LANES)
    moved, walls, where = first_call(x, wall_mask)
    branches = [functools.partial(second_call, block) for block in range(SPACE)]
    out = lax.switch(where[0], branches, moved, walls)
    return out.reshape(distribution.shape)


def solution(mesh):
    placed = (P("vel", "space", None), P("space", None))
    return jax.shard_map(
        shards, mesh=mesh, in_specs=placed, out_specs=P("vel", "space", None), check_vma=False
    )
```

time: 467 us -> 144 us (0.31)
  the two profiles are of different devices: /device:TPU:40 before, /device:TPU:113 now
where the time goes in v1:
time: 144 us
  Pallas kernels  140 us (97%)
  local copies, waits for them, and re-layouts  3.37 us (2%)
    pallas_call x1, Pallas kernels, second_call(): pl.pallas_call(functools.partial(second_kernel, block), out_shape=jax.Sha...  105 us
    pallas_call x1, Pallas kernels, first_call(): pl.pallas_call(first_kernel, out_shape=(jax.ShapeDtypeStruct((COLS, ROWS,...  34.5 us
    unnamed x5, local copies, waits for them, and re-layouts  3.37 us

profile of v1, /device:TPU:113, one launch (start us, length us, event | category | flops | bytes accessed | tf_op | source)
XLA Modules:
  0.0 143.9 jit_solution(4060902798090741888)
XLA Ops:
  0.0 0.0 copy-start
  0.0 1.5 %copy-done = f32[864,4,128]{2,1,0:T(4,128)S(1)} copy-done((f32[864,4,128]{2,1,0:T(4,128)S(1)}, f32[864,4,128]{2,1,0:T(4,128)}, u32[]{:S(2)}) %copy-start) | copy-done | bytes 1769496
  1.5 0.0 copy-start.1
  1.5 0.7 copy-done.1
  2.2 34.5 %first.1 = (f32[4,864,128]{2,1,0:T(8,128)S(1)}, f32[8,128]{1,0:T(8,128)S(1)}, s32[1]{0:T(128)}) custom-call(f32[3456,128]{1,0:T(8,128)S(1)} %bitcast.18, s32[4,128]{1,0:T(4,128)S(1)} %copy-done.1), custom_call_target="tpu_custom_call" | custom-call | tf_op jit(solution)/shard_map/first/pallas_call | solution.py:494
  37.3 105.4 %conditional.1 = (f32[864,4,128]{2,1,0:T(4,128)S(1)}) conditional(s32[]{:T(128)} %bitcast.17, (f32[4,864,128]{2,1,0:T(8,128)S(1)}, f32[8,128]{1,0:T(8,128)S(1)}) %tuple.69, (f32[4,864,128]{2,1,0:T(8,128)S(1)}, f32[8,128]{1,0:T(8,128)S(1)}) %tuple.69, (f32[4,864,128]{2,1,0:T(8,128)S(1)}, ...), branch_computations={%region_0.0_spmd, %region_1.0_spmd, %region_2.0_spmd, %region_3.0_... | conditional | bytes 8 | solution.py:564
  37.5 105.1 %second11.1 = f32[3456,128]{1,0:T(8,128)S(1)} custom-call(f32[4,864,128]{2,1,0:T(8,128)S(1)} %get-tuple-element.109.moved_ref, f32[8,128]{1,0:T(8,128)S(1)} %get-tuple-element.110.walls), custom_call_target="tpu_custom_call" | custom-call | tf_op jit(solution)/shard_map/cond/branch_11_fun/second11/pallas_call | solution.py:527
  142.7 1.2 copy.36
Async XLA Ops:
  0.0 1.5 %copy-start = (f32[864,4,128]{2,1,0:T(4,128)S(1)}, f32[864,4,128]{2,1,0:T(4,128)}, u32[]{:S(2)}) copy-start(f32[864,4,128]{2,1,0:T(4,128)} %param.18) | copy-start | bytes 5308420
  1.5 0.7 copy-start.1

commit v2 on v1

--- a/solution.py
+++ b/solution.py
@@ -61,7 +61,7 @@
 
     def z(self, t):
         sub = lax.broadcasted_iota(jnp.int32, (8, LANES), 0).astype(F32)
-        return ((sub + (8 * t + 0.5)) * NODE - 4.5) * (1 - 2 * self.pos).astype(F32)
+        return ((sub + 8.0 * jnp.asarray(t, F32) + 0.5) * NODE - 4.5) * (1 - 2 * self.pos).astype(F32)
 
 
 def at(row):
@@ -79,26 +79,26 @@
         for t in range(3):
             rows = at((g * 12 + r) * 24 + 8 * t)
             lines = {l: field[l, rows, :] for l in range(flows[0], flows[-1] + 3)}
+            nears = {l: lines[l + 2] - 0.25 * pltpu.roll(lines[l + 2], shift, 1) for l in flows}
+            nears = {l: pltpu.roll(nears[l], shift, 1) for l in flows}
             for l in flows:
-                own = lines[l + 2]
-                near = own - 0.25 * pltpu.roll(own, shift, 1)
-                near = pltpu.roll(near, shift, 1)
                 moved[l, rows, :] = (
-                    keep * own
+                    keep * lines[l + 2]
                     + (2.0 * alpha) * (lines[l + 1] - 0.25 * lines[l])
-                    + (2.0 * beta) * near
+                    + (2.0 * beta) * nears[l]
                 )
         return carry
 
-    lax.fori_loop(first, first + count, run, 0)
+    lax.fori_loop(first, first + count, run, 0, unroll=6)
 
 
 def moments(place, field, part, sums, z_sums):
     def group(g, carry):
         speed, half, y0, slope = place.group(g)
         x = place.vx(speed)
-        for t in range(3):
-
+        z_sums[...] = jnp.zeros_like(z_sums)
+
+        def tile(t, carry):
             def run(r, acc):
                 y = y0 + slope * r.astype(F32)
                 rows = at((g * 12 + r) * 24 + 8 * t)
@@ -111,19 +111,18 @@
                     out += [acc[4 * l] + f0, acc[4 * l + 1] + f1, acc[4 * l + 2] + f2, acc[4 * l + 3] + f3]
                 return tuple(out)
 
-            acc = lax.fori_loop(0, 12, run, (jnp.zeros((8, LANES), F32),) * 16)
+            acc = lax.fori_loop(0, 12, run, (jnp.zeros((8, LANES), F32),) * 16, unroll=12)
             z = place.z(t)
             for l in range(COLS):
                 a, b, c, d = acc[4 * l : 4 * l + 4]
                 za = z * a
                 zb = z * b
                 zza = z * za
-                terms = [a, b, c, d, za, zb, z * c, zza, z * zb, z * zza]
-                for m, term in enumerate(terms):
-                    if t == 0:
-                        z_sums[l, m] = term
-                    else:
-                        z_sums[l, m] = z_sums[l, m] + term
+                for m, term in enumerate([a, b, c, d, za, zb, z * c, zza, z * zb, z * zza]):
+                    z_sums[l, m] = z_sums[l, m] + term
+            return carry
+
+        lax.fori_loop(0, 3, tile, 0)
         for l in range(COLS):
             a, b, c, d, za, zb, zc, zza, zzb, zzza = [z_sums[l, m] for m in range(10)]
             xx = x * x
@@ -189,7 +188,7 @@
     return jnp.broadcast_to(row, (8, LANES))
 
 
-def relax(place, load, store, params, p, table):
+def relax(place, load, store, params, p, table, groups=(0, 3)):
     ux, uy, uz, half_t, inv_t, peak, kx, ky, kz, keep = [params[p, pl.ds(i, 1), :] for i in range(10)]
     z_exp, z_dot, z_square = [], [], []
     for t in range(3):
@@ -198,21 +197,20 @@
         z_dot.append(c * spread(kz))
         z_square.append(c * c * spread(inv_t))
     keep8 = spread(keep)
-    for g in range(3):
+    def group(g, carry):
         speed, half, y0, slope = place.group(g)
         cx = place.vx(speed) - ux
         for part in range(2):
             index = lax.broadcasted_iota(jnp.int32, (8, LANES), 0).astype(F32) + 8.0 * part
             cy = (y0 + slope * index) - spread(uy)
             square = spread(cx * cx) + cy * cy
-            rows = pl.ds(16 * g + 8 * part, 8)
+            rows = pl.ds(8 * part, 8)
             table[0, rows, :] = spread(peak) * jnp.exp(-square * spread(half_t))
             table[1, rows, :] = spread(cx * kx) + cy * spread(ky)
             table[2, rows, :] = square * spread(inv_t) - 5.0
-    for g in range(3):
 
         def run(r, carry):
-            line = pl.ds(16 * g + r, 1)
+            line = pl.ds(r, 1)
             amp = spread(table[0, line, :])
             dot = spread(table[1, line, :])
             square = spread(table[2, line, :])
@@ -223,7 +221,9 @@
                 store(row, keep8 * old + (amp * z_exp[t]) * shape)
             return carry
 
-        lax.fori_loop(0, 12, run, 0, unroll=2)
+        return lax.fori_loop(0, 12, run, carry, unroll=12)
+
+    lax.fori_loop(groups[0], groups[1], group, 0)
 
 
 def flip8(x):
@@ -233,10 +233,14 @@
     return jnp.where(sub % 2 < 1, pltpu.roll(x, 7, 0), pltpu.roll(x, 1, 0))
 
 
-def first_kernel(x_ref, mask_ref, moved, walls, where, raw, field, note, hear, in_sem, ssem, rsem, nsem, hsem):
+def first_kernel(
+    x_ref, mask_ref, moved, walls, where, raw, mask_in, field, note, hear, in_sem, mask_sem, ssem, rsem, nsem, hsem
+):
     place = Place()
     s, v = place.s, place.v
     span = CROWS * COLS
+    mask_copy = pltpu.make_async_copy(mask_ref, mask_in, mask_sem)
+    mask_copy.start()
     loads = [
         pltpu.make_async_copy(x_ref.at[pl.ds(c * span, span)], raw.at[pl.ds(c * span, span)], in_sem.at[c])
         for c in range(CHUNKS)
@@ -251,7 +255,8 @@
     for device in [place.up] + mates + cross:
         signal(barrier, device)
 
-    mask = mask_ref[...].astype(F32)
+    mask_copy.wait()
+    mask = mask_in[...].astype(F32)
     has = [jnp.broadcast_to(jnp.max(mask[i : i + 1, :], axis=1, keepdims=True), (1, LANES)) for i in range(COLS)]
     first = has[0]
     second = (1.0 - has[0]) * has[1]
@@ -267,23 +272,23 @@
                 field[l + 2, at(row), :] = raw[pl.ds(row * COLS + place.layer(l), 8, stride=COLS), :]
             return carry
 
-        lax.fori_loop(0, CROWS // 8, body, 0, unroll=2)
-
+        lax.fori_loop(0, CROWS // 8, body, 0, unroll=6)
+
+    words = [remote(note.at[0], hear.at[i], nsem.at[i], hsem.at[i], mates[i]) for i in range(3)]
     sends = []
     for c in range(CHUNKS):
         loads[c].wait()
         split((2, 3), c)
         if c == 0:
             pl.semaphore_wait(barrier, 7)
+            for copy in words:
+                copy.start()
         rows = pl.ds(c * CROWS, CROWS)
         copy = remote(
             field.at[pl.ds(4, 2), rows], field.at[pl.ds(0, 2), rows], ssem.at[c], rsem.at[c], place.down
         )
         copy.start()
         sends.append(copy)
-    words = [remote(note.at[0], hear.at[i], nsem.at[i], hsem.at[i], mates[i]) for i in range(3)]
-    for copy in words:
-        copy.start()
     for c in range(CHUNKS):
         split((0, 1), c)
     for copy in words:
@@ -298,13 +303,13 @@
         return carry
 
     lax.fori_loop(0, 3, later, 0)
+    for c in range(CHUNKS):
+        sends[c].wait_recv()
+        transport(place, field, moved, (0, 1), c // 2, 6 * (c % 2), 6)
     for copy in more:
         copy.wait_recv()
     total = note[1] + hear[3] + hear[4] + hear[5]
     where[0] = jnp.max(total).astype(jnp.int32)
-    for c in range(CHUNKS):
-        sends[c].wait_recv()
-        transport(place, field, moved, (0, 1), c // 2, 6 * (c % 2), 6)
     for copy in sends + words + more:
         copy.wait_send()
 
@@ -314,12 +319,12 @@
     moved_ref,
     walls,
     out,
-    one,
+    states,
     halo,
     field,
-    two,
     slab,
     mirror,
+    relay,
     part,
     z_sums,
     sums,
@@ -329,17 +334,24 @@
     edge,
     table,
     in_sem,
-    hsem,
-    xsem,
+    halo_sem,
+    out_sem,
+    back_sem,
+    relay_sem,
+    pass_sem,
     psem,
     esem,
 ):
     place = Place()
     s, v = place.s, place.v
-    load = pltpu.make_async_copy(moved_ref, one, in_sem)
+    load = pltpu.make_async_copy(moved_ref, states.at[0], in_sem)
     load.start()
     after = (block + 1) % SPACE
-    near_wall = jnp.logical_or(s == block, s == after)
+    sides = ((block + 4) % SPACE, (block + 12) % SPACE)
+    beyond = (after + (8 if block % 4 < 3 else 4)) % SPACE
+    in_block, in_after, in_beyond = s == block, s == after, s == beyond
+    in_sides = jnp.logical_or(s == sides[0], s == sides[1])
+    one_more = jnp.logical_or(in_sides, jnp.logical_or(in_after, in_beyond))
     partner = (s, 15 - v)
     peer = (s, v + 1 - 2 * place.core)
     chips = [lax.rem(place.chip + i, 8) for i in range(1, 8)]
@@ -349,12 +361,19 @@
     for device in [place.up, peer] + mates:
         signal(barrier, device)
 
-    @pl.when(near_wall)
+    @pl.when(in_block)
     def _():
-        signal(barrier, partner)
+        for device in [partner, (sides[0], 15 - v), (sides[1], 15 - v)]:
+            signal(barrier, device)
+        pl.semaphore_wait(barrier, 12)
+
+    @pl.when(one_more)
+    def _():
+        source = jnp.where(in_sides, block, jnp.where(in_after, beyond, after))
+        signal(barrier, (source, jnp.where(in_after, 15 - v, v)))
         pl.semaphore_wait(barrier, 10)
 
-    @pl.when(jnp.logical_not(near_wall))
+    @pl.when(jnp.logical_not(jnp.logical_or(in_block, one_more)))
     def _():
         pl.semaphore_wait(barrier, 9)
 
@@ -370,35 +389,125 @@
             slab[k, 1, rows, :] = jnp.where(at0, lines[1], jnp.where(at1, lines[2], lines[3]))
             return carry
 
-        def put(i, carry):
-            rows = at(8 * i)
-            back = at(ROWS - 8 - 8 * i)
-            near = flip8(mirror[k, 0, back, :])
-            far = flip8(mirror[k, 1, back, :])
-            for l in range(COLS):
-                new = jnp.where(spread(walls[4 + l : 5 + l, :]) > 0.5, near, far)
-                line = place.layer(l)
-                state[line, rows, :] = jnp.where(spread(walls[l : l + 1, :]) > 0.5, new, state[line, rows, :])
-            return carry
-
-        @pl.when(s == block)
+        def put(first, count):
+            def body(i, carry):
+                back = at(first + 8 * i)
+                rows = at(ROWS - 8 - first - 8 * i)
+                near = flip8(mirror[k, 0, back, :])
+                far = flip8(mirror[k, 1, back, :])
+                for l in range(COLS):
+                    new = jnp.where(spread(walls[4 + l : 5 + l, :]) > 0.5, near, far)
+                    line = place.layer(l)
+                    state[line, rows, :] = jnp.where(spread(walls[l : l + 1, :]) > 0.5, new, state[line, rows, :])
+                return carry
+
+            lax.fori_loop(0, count // 8, body, 0, unroll=3)
+
+        def direct(c):
+            rows = pl.ds(96 * c, 96)
+            return remote(
+                slab.at[k, :, rows], mirror.at[k, :, rows], out_sem.at[k, c], back_sem.at[k, c], partner
+            )
+
+        def lead(side, c):
+            rows = pl.ds(288 * (side + 1) + 96 * c, 96)
+            return remote(
+                slab.at[k, :, rows],
+                relay.at[k, :, pl.ds(96 * c, 96)],
+                out_sem.at[k, 3 * side + 3 + c],
+                relay_sem.at[k, c],
+                (sides[side], v),
+            )
+
+        def follow(side, c):
+            rows = pl.ds(288 * (side + 1) + 96 * c, 96)
+            return remote(
+                relay.at[k, :, pl.ds(96 * c, 96)],
+                mirror.at[k, :, rows],
+                pass_sem.at[k, c],
+                back_sem.at[k, 3 * side + 3 + c],
+                (block, 15 - v),
+            )
+
+        def lead_far(c):
+            return remote(
+                slab.at[k, 0, pl.ds(288 * c, 288)],
+                relay.at[k, c // 2, pl.ds(288 * (c % 2), 288)],
+                out_sem.at[k, c],
+                relay_sem.at[k, c],
+                (beyond, v),
+            )
+
+        def follow_far(c):
+            return remote(
+                relay.at[k, c // 2, pl.ds(288 * (c % 2), 288)],
+                mirror.at[k, 0, pl.ds(288 * c, 288)],
+                pass_sem.at[k, c],
+                back_sem.at[k, c],
+                (after, 15 - v),
+            )
+
+        @pl.when(in_block)
         def _():
-            lax.fori_loop(0, ROWS // 8, cut, 0)
-            copy = remote(slab.at[k], mirror.at[k], xsem.at[k, 0], xsem.at[k, 1], partner)
-            copy.start()
-            copy.wait()
-            lax.fori_loop(0, ROWS // 8, put, 0)
-
-        @pl.when(s == after)
+            def depart(c, carry):
+                def each(side, carry):
+                    first = 36 * side + 12 * c
+                    return lax.fori_loop(0, 12, lambda i, carry: cut(first + i, carry), carry, unroll=3)
+
+                lax.fori_loop(0, 3, each, carry)
+                lead(0, c).start()
+                lead(1, c).start()
+                direct(c).start()
+                return carry
+
+            lax.fori_loop(0, 3, depart, 0)
+            def arrive(c, carry):
+                for side in range(3):
+                    (follow(side - 1, c) if side else direct(c)).wait_recv()
+
+                def each(side, carry):
+                    put(288 * side + 96 * c, 96)
+                    return carry
+
+                return lax.fori_loop(0, 3, each, carry)
+
+            lax.fori_loop(0, 3, arrive, 0)
+            for c in range(3):
+                direct(c).wait_send()
+                lead(0, c).wait_send()
+                lead(1, c).wait_send()
+
+        for side in range(2):
+
+            @pl.when(s == sides[side])
+            def _():
+                for c in range(3):
+                    lead(side, c).wait_recv()
+                    follow(side, c).start()
+                for c in range(3):
+                    follow(side, c).wait_send()
+
+        @pl.when(in_after)
         def _():
-            lax.fori_loop(0, ROWS // 8, cut, 0)
             mirror[k, 1] = jnp.zeros((ROWS, LANES), F32)
-            copy = remote(slab.at[k, 0], mirror.at[k, 0], xsem.at[k, 0], xsem.at[k, 1], partner)
-            copy.start()
-            copy.wait()
-            lax.fori_loop(0, ROWS // 8, put, 0)
-
-    def total(k):
+            lax.fori_loop(0, ROWS // 8, cut, 0, unroll=3)
+            for c in range(3):
+                lead_far(c).start()
+            for c in range(3):
+                follow_far(c).wait_recv()
+            put(0, ROWS)
+            for c in range(3):
+                lead_far(c).wait_send()
+
+        @pl.when(in_beyond)
+        def _():
+            for c in range(3):
+                lead_far(c).wait_recv()
+                follow_far(c).start()
+            for c in range(3):
+                follow_far(c).wait_send()
+
+    def total(k, between):
         mine = pl.ds(2 * place.core, 2)
         first = remote(
             sums.at[k, pl.ds(2 - 2 * place.core, 2)], swap.at[k], psem.at[k, 0, 0], psem.at[k, 1, 0], peer
@@ -413,6 +522,7 @@
             )
             copy.start()
             outs.append(copy)
+        between()
         for copy in outs:
             copy.wait_recv()
         whole = gather[k, 0]
@@ -424,69 +534,95 @@
         last = remote(params.at[k, mine], params.at[k, mine], psem.at[k, 0, 8], psem.at[k, 1, 8], peer)
         last.start()
         last.wait_recv()
-        return [first, last] + outs
-
-    reflect(one, 0)
-    hand = remote(one.at[pl.ds(2, 2)], halo, hsem.at[0], hsem.at[1], place.down)
-    hand.start()
-    moments(place, one, part, sums.at[0], z_sums)
-    open_copies = total(0)
+        for copy in [first, last] + outs:
+            copy.wait_send()
+
+    def hand(g):
+        rows = pl.ds(288 * g, 288)
+        return remote(
+            states.at[0, pl.ds(2, 2), rows], halo.at[:, rows], halo_sem.at[0, g], halo_sem.at[1, g], place.down
+        )
+
+    early = jnp.logical_or(in_block, in_after)
     tell = remote(
         params.at[0, pl.ds(2 * place.pos, 2)], edge, esem.at[0], esem.at[1], place.down
     )
-    tell.start()
-
-    def own(l, carry):
-        def load_row(row):
-            return one[l, at(row), :]
-
-        def store_row(row, value):
-            field[l + 2, at(row), :] = value
-
-        relax(place, load_row, store_row, params.at[0], place.layer(l), table)
+
+    def hand_on():
+        for g in range(3):
+            hand(g).start()
+
+    def middle():
+        tell.start()
+        pl.when(jnp.logical_not(early))(hand_on)
+
+        def own(l, carry):
+            def load_row(row):
+                return states[0, l, at(row), :]
+
+            def store_row(row, value):
+                field[l + 2, at(row), :] = value
+
+            relax(place, load_row, store_row, params.at[0], place.layer(l), table)
+            return carry
+
+        lax.fori_loop(0, COLS, own, 0)
+
+        def later(g, carry):
+            transport(place, field, states.at[1], (2, 3), g, 0, 12)
+            return carry
+
+        lax.fori_loop(0, 3, later, 0)
+        tell.wait_recv()
+
+        def chunk(g, carry):
+            hand(g).wait_recv()
+
+            def beside(l, carry):
+                def load_row(row):
+                    return halo[l, at(row), :]
+
+                def store_row(row, value):
+                    field[l, at(row), :] = value
+
+                relax(
+                    place, load_row, store_row, edge, jnp.where(place.pos == 1, l, 1 - l), table, (g, g + 1)
+                )
+                return carry
+
+            lax.fori_loop(0, 2, beside, 0)
+            transport(place, field, states.at[1], (0, 1), g, 0, 12)
+            return carry
+
+        lax.fori_loop(0, 3, chunk, 0)
+
+    def last():
+        def end(l, carry):
+            layer = place.layer(l)
+
+            def load_row(row):
+                return states[1, l, at(row), :]
+
+            def store_row(row, value):
+                out[pl.ds(row * COLS + layer, 8, stride=COLS), :] = value
+
+            relax(place, load_row, store_row, params.at[1], layer, table)
+            return carry
+
+        lax.fori_loop(0, COLS, end, 0)
+
+    def step(k, carry):
+        reflect(states.at[k], k)
+        moments(place, states.at[k], part, sums.at[k], z_sums)
+        total(k, lambda: pl.when(jnp.logical_and(early, k == 0))(hand_on))
+        pl.when(k == 0)(middle)
+        pl.when(k == 1)(last)
         return carry
 
-    lax.fori_loop(0, COLS, own, 0)
-    tell.wait_recv()
-    hand.wait_recv()
-
-    def beside(l, carry):
-        def load_row(row):
-            return halo[l, at(row), :]
-
-        def store_row(row, value):
-            field[l, at(row), :] = value
-
-        relax(place, load_row, store_row, edge, jnp.where(place.pos == 1, l, 1 - l), table)
-        return carry
-
-    lax.fori_loop(0, 2, beside, 0)
-
-    def step(g, carry):
-        transport(place, field, two, (0, 1, 2, 3), g, 0, 12)
-        return carry
-
-    lax.fori_loop(0, 3, step, 0)
-
-    reflect(two, 1)
-    moments(place, two, part, sums.at[1], z_sums)
-    open_copies += total(1)
-
-    def end(l, carry):
-        layer = place.layer(l)
-
-        def load_row(row):
-            return two[l, at(row), :]
-
-        def store_row(row, value):
-            out[pl.ds(row * COLS + layer, 8, stride=COLS), :] = value
-
-        relax(place, load_row, store_row, params.at[1], layer, table)
-        return carry
-
-    lax.fori_loop(0, COLS, end, 0)
-    for copy in open_copies + [hand, tell]:
-        copy.wait_send()
+    lax.fori_loop(0, 2, step, 0)
+    tell.wait_send()
+    for g in range(3):
+        hand(g).wait_send()
 
 
 def first_call(x, mask):
@@ -498,7 +634,7 @@
             jax.ShapeDtypeStruct((8, LANES), F32),
             jax.ShapeDtypeStruct((1,), jnp.int32),
         ),
-        in_specs=[pl.BlockSpec(memory_space=pl.ANY), pl.BlockSpec(memory_space=pltpu.VMEM)],
+        in_specs=[pl.BlockSpec(memory_space=pltpu.HBM), pl.BlockSpec(memory_space=pltpu.HBM)],
         out_specs=(
             pl.BlockSpec(memory_space=pltpu.VMEM),
             pl.BlockSpec(memory_space=pltpu.VMEM),
@@ -506,17 +642,19 @@
         ),
         scratch_shapes=[
             pltpu.VMEM((ROWS * COLS, LANES), F32),
+            pltpu.VMEM((COLS, LANES), jnp.int32),
             pltpu.VMEM((COLS + 2, ROWS, LANES), F32),
             pltpu.VMEM((2, 8, LANES), F32),
             pltpu.VMEM((6, 8, LANES), F32),
             dma((CHUNKS,)),
+            dma,
             dma((CHUNKS,)),
             dma((CHUNKS,)),
             dma((6,)),
             dma((6,)),
         ],
         compiler_params=pltpu.CompilerParams(
-            collective_id=0, has_side_effects=True, vmem_limit_bytes=24 << 20
+            collective_id=0, has_side_effects=True, vmem_limit_bytes=60 << 20
         ),
         name="first",
     )(x, mask)
@@ -530,12 +668,12 @@
         in_specs=[pl.BlockSpec(memory_space=pl.ANY), pl.BlockSpec(memory_space=pltpu.VMEM)],
         out_specs=pl.BlockSpec(memory_space=pltpu.VMEM),
         scratch_shapes=[
-            pltpu.VMEM((COLS, ROWS, LANES), F32),
+            pltpu.VMEM((2, COLS, ROWS, LANES), F32),
             pltpu.VMEM((2, ROWS, LANES), F32),
             pltpu.VMEM((COLS + 2, ROWS, LANES), F32),
-            pltpu.VMEM((COLS, ROWS, LANES), F32),
             pltpu.VMEM((2, 2, ROWS, LANES), F32),
             pltpu.VMEM((2, 2, ROWS, LANES), F32),
+            pltpu.VMEM((2, 2, 576, LANES), F32),
             pltpu.VMEM((COLS, 13, 8, LANES), F32),
             pltpu.VMEM((COLS, 10, 8, LANES), F32),
             pltpu.VMEM((2, COLS, 16, LANES), F32),
@@ -543,10 +681,13 @@
             pltpu.VMEM((2, 8, 2, 16, LANES), F32),
             pltpu.VMEM((2, COLS, 16, LANES), F32),
             pltpu.VMEM((2, 16, LANES), F32),
-            pltpu.VMEM((3, 48, LANES), F32),
+            pltpu.VMEM((3, 16, LANES), F32),
             dma,
-            dma((2,)),
-            dma((2, 2)),
+            dma((2, 3)),
+            dma((2, 9)),
+            dma((2, 9)),
+            dma((2, 3)),
+            dma((2, 3)),
             dma((2, 2, 9)),
             dma((2,)),
         ],

time: 144 us -> 115 us (0.80)
  the two profiles are of different devices: /device:TPU:113 before, /device:TPU:217 now
where the time goes in v2:
time: 115 us
  Pallas kernels  113 us (98%)
  local copies, waits for them, and re-layouts  1.21 us (1%)
    pallas_call x1, Pallas kernels, second_call(): pl.pallas_call(functools.partial(second_kernel, block), out_shape=jax.Sha...  89.9 us
    pallas_call x1, Pallas kernels, first_call(): pl.pallas_call(first_kernel, out_shape=(jax.ShapeDtypeStruct((COLS, ROWS,...  22.8 us

profile of v2, /device:TPU:217, one launch (start us, length us, event | category | flops | bytes accessed | tf_op | source)
XLA Modules:
  0.0 114.8 jit_solution(2330687277681248554)
XLA Ops:
  0.0 22.8 %first.1 = (f32[4,864,128]{2,1,0:T(8,128)S(1)}, f32[8,128]{1,0:T(8,128)S(1)}, s32[1]{0:T(128)}) custom-call(f32[3456,128]{1,0:T(8,128)} %bitcast.34, s32[4,128]{1,0:T(4,128)} %mask_ref.1), custom_call_target="tpu_custom_call" | custom-call | tf_op jit(solution)/shard_map/first/pallas_call | solution.py:630
  23.4 90.2 %conditional.1 = (f32[864,4,128]{2,1,0:T(4,128)S(1)}) conditional(s32[]{:T(128)} %bitcast.17, (f32[4,864,128]{2,1,0:T(8,128)S(1)}, f32[8,128]{1,0:T(8,128)S(1)}) %tuple.69, (f32[4,864,128]{2,1,0:T(8,128)S(1)}, f32[8,128]{1,0:T(8,128)S(1)}) %tuple.69, (f32[4,864,128]{2,1,0:T(8,128)S(1)}, ...), branch_computations={%region_0.0_spmd, %region_1.0_spmd, %region_2.0_spmd, %region_3.0_... | conditional | bytes 8 | solution.py:705
  23.7 89.9 %second14.1 = f32[3456,128]{1,0:T(8,128)S(1)} custom-call(f32[4,864,128]{2,1,0:T(8,128)S(1)} %get-tuple-element.115.moved_ref, f32[8,128]{1,0:T(8,128)S(1)} %get-tuple-element.116.walls), custom_call_target="tpu_custom_call" | custom-call | tf_op jit(solution)/shard_map/cond/branch_14_fun/second14/pallas_call | solution.py:665
  113.6 1.2 %copy.36 = f32[864,4,128]{2,1,0:T(4,128)} copy(f32[864,4,128]{2,1,0:T(4,128)S(1)} %get-tuple-element.125) | data formatting | bytes 3538944

commit v3 on v2

--- a/solution.py
+++ b/solution.py
@@ -89,10 +89,10 @@
                 )
         return carry
 
-    lax.fori_loop(first, first + count, run, 0, unroll=6)
-
-
-def moments(place, field, part, sums, z_sums):
+    lax.fori_loop(0, count, lambda i, carry: run(first + i, carry), 0, unroll=4)
+
+
+def moments(place, field, walls, part, sums, z_sums):
     def group(g, carry):
         speed, half, y0, slope = place.group(g)
         x = place.vx(speed)
@@ -111,7 +111,7 @@
                     out += [acc[4 * l] + f0, acc[4 * l + 1] + f1, acc[4 * l + 2] + f2, acc[4 * l + 3] + f3]
                 return tuple(out)
 
-            acc = lax.fori_loop(0, 12, run, (jnp.zeros((8, LANES), F32),) * 16, unroll=12)
+            acc = lax.fori_loop(0, 12, run, (jnp.zeros((8, LANES), F32),) * 16, unroll=6)
             z = place.z(t)
             for l in range(COLS):
                 a, b, c, d = acc[4 * l : 4 * l + 4]
@@ -148,7 +148,11 @@
     part[...] = jnp.zeros_like(part)
     lax.fori_loop(0, 3, group, 0)
     for l in range(COLS):
-        rows = [jnp.sum(part[l, m], axis=0, keepdims=True) * WEIGHT for m in range(13)]
+        flip = WEIGHT * (1.0 - 2.0 * walls[pl.ds(place.layer(l), 1), :])
+        rows = [
+            jnp.sum(part[l, m], axis=0, keepdims=True) * (flip if m in (1, 7, 8, 10) else WEIGHT)
+            for m in range(13)
+        ]
         sums[place.layer(l)] = jnp.concatenate(rows + [jnp.zeros((3, LANES), F32)], axis=0)
 
 
@@ -188,7 +192,7 @@
     return jnp.broadcast_to(row, (8, LANES))
 
 
-def relax(place, load, store, params, p, table, groups=(0, 3)):
+def relax(place, load, store, params, p, table, groups=(0, 3), first=0, count=12):
     ux, uy, uz, half_t, inv_t, peak, kx, ky, kz, keep = [params[p, pl.ds(i, 1), :] for i in range(10)]
     z_exp, z_dot, z_square = [], [], []
     for t in range(3):
@@ -221,7 +225,7 @@
                 store(row, keep8 * old + (amp * z_exp[t]) * shape)
             return carry
 
-        return lax.fori_loop(0, 12, run, carry, unroll=12)
+        return lax.fori_loop(0, count, lambda i, carry: run(first + i, carry), carry, unroll=4)
 
     lax.fori_loop(groups[0], groups[1], group, 0)
 
@@ -347,11 +351,14 @@
     load = pltpu.make_async_copy(moved_ref, states.at[0], in_sem)
     load.start()
     after = (block + 1) % SPACE
-    sides = ((block + 4) % SPACE, (block + 12) % SPACE)
-    beyond = (after + (8 if block % 4 < 3 else 4)) % SPACE
-    in_block, in_after, in_beyond = s == block, s == after, s == beyond
-    in_sides = jnp.logical_or(s == sides[0], s == sides[1])
-    one_more = jnp.logical_or(in_sides, jnp.logical_or(in_after, in_beyond))
+
+    def at_wall(place):
+        return jnp.logical_or(place == block, place == after)
+
+    near_wall = at_wall(s)
+    sides = (lax.rem(s + 4, SPACE), lax.rem(s + 12, SPACE))
+    relaying = (at_wall(sides[1]), at_wall(sides[0]))
+    one_more = jnp.logical_or(relaying[0], relaying[1])
     partner = (s, 15 - v)
     peer = (s, v + 1 - 2 * place.core)
     chips = [lax.rem(place.chip + i, 8) for i in range(1, 8)]
@@ -361,7 +368,7 @@
     for device in [place.up, peer] + mates:
         signal(barrier, device)
 
-    @pl.when(in_block)
+    @pl.when(near_wall)
     def _():
         for device in [partner, (sides[0], 15 - v), (sides[1], 15 - v)]:
             signal(barrier, device)
@@ -369,15 +376,33 @@
 
     @pl.when(one_more)
     def _():
-        source = jnp.where(in_sides, block, jnp.where(in_after, beyond, after))
-        signal(barrier, (source, jnp.where(in_after, 15 - v, v)))
+        signal(barrier, (jnp.where(relaying[0], sides[1], sides[0]), v))
         pl.semaphore_wait(barrier, 10)
 
-    @pl.when(jnp.logical_not(jnp.logical_or(in_block, one_more)))
+    @pl.when(jnp.logical_not(jnp.logical_or(near_wall, one_more)))
     def _():
         pl.semaphore_wait(barrier, 9)
 
+    @pl.when(s == after)
+    def _():
+        mirror[:, 1] = jnp.zeros((2, ROWS, LANES), F32)
+
     load.wait()
+
+    def hand(g, c):
+        rows = pl.ds(288 * g + 96 * c, 96)
+        return remote(
+            states.at[0, pl.ds(2, 2), rows],
+            halo.at[:, rows],
+            halo_sem.at[0, 3 * g + c],
+            halo_sem.at[1, 3 * g + c],
+            place.down,
+        )
+
+    def hand_on():
+        for c in (2, 1, 0):
+            for g in (2, 1, 0):
+                hand(g, c).start()
 
     def reflect(state, k):
         def cut(i, carry):
@@ -403,109 +428,99 @@
 
             lax.fori_loop(0, count // 8, body, 0, unroll=3)
 
-        def direct(c):
+        def direct(c, j):
             rows = pl.ds(96 * c, 96)
             return remote(
-                slab.at[k, :, rows], mirror.at[k, :, rows], out_sem.at[k, c], back_sem.at[k, c], partner
+                slab.at[k, j, rows], mirror.at[k, j, rows], out_sem.at[k, j, c], back_sem.at[k, j, c], partner
             )
 
-        def lead(side, c):
-            rows = pl.ds(288 * (side + 1) + 96 * c, 96)
+        def lead(side, c, j):
             return remote(
-                slab.at[k, :, rows],
-                relay.at[k, :, pl.ds(96 * c, 96)],
-                out_sem.at[k, 3 * side + 3 + c],
-                relay_sem.at[k, c],
+                slab.at[k, j, pl.ds(288 * (side + 1) + 96 * c, 96)],
+                relay.at[k, j, pl.ds(96 * c, 96)],
+                out_sem.at[k, j, 3 * side + 3 + c],
+                relay_sem.at[k, j, c],
                 (sides[side], v),
             )
 
-        def follow(side, c):
-            rows = pl.ds(288 * (side + 1) + 96 * c, 96)
+        def follow(side, c, j):
             return remote(
-                relay.at[k, :, pl.ds(96 * c, 96)],
-                mirror.at[k, :, rows],
-                pass_sem.at[k, c],
-                back_sem.at[k, 3 * side + 3 + c],
-                (block, 15 - v),
+                relay.at[k, j, pl.ds(96 * c, 96)],
+                mirror.at[k, j, pl.ds(288 * (side + 1) + 96 * c, 96)],
+                pass_sem.at[k, j, c],
+                back_sem.at[k, j, 3 * side + 3 + c],
+                (sides[1 - side], 15 - v),
             )
 
-        def lead_far(c):
-            return remote(
-                slab.at[k, 0, pl.ds(288 * c, 288)],
-                relay.at[k, c // 2, pl.ds(288 * (c % 2), 288)],
-                out_sem.at[k, c],
-                relay_sem.at[k, c],
-                (beyond, v),
-            )
-
-        def follow_far(c):
-            return remote(
-                relay.at[k, c // 2, pl.ds(288 * (c % 2), 288)],
-                mirror.at[k, 0, pl.ds(288 * c, 288)],
-                pass_sem.at[k, c],
-                back_sem.at[k, c],
-                (after, 15 - v),
-            )
-
-        @pl.when(in_block)
-        def _():
+        def ways(c, j, act):
+            act(lead(0, c, j))
+            act(lead(1, c, j))
+            act(direct(c, j))
+
+        def each_slot(both, act):
+            act(0)
+            pl.when(both)(lambda: act(1))
+
+        def send():
             def depart(c, carry):
                 def each(side, carry):
                     first = 36 * side + 12 * c
                     return lax.fori_loop(0, 12, lambda i, carry: cut(first + i, carry), carry, unroll=3)
 
                 lax.fori_loop(0, 3, each, carry)
-                lead(0, c).start()
-                lead(1, c).start()
-                direct(c).start()
+                each_slot(s == block, lambda j: ways(c, j, lambda copy: copy.start()))
                 return carry
 
-            lax.fori_loop(0, 3, depart, 0)
+            pl.when(near_wall)(lambda: lax.fori_loop(0, 3, depart, None))
+
+        def relays():
+            for side in range(2):
+
+                def forward(c, carry):
+                    def one(j):
+                        lead(side, c, j).wait_recv()
+                        follow(side, c, j).start()
+
+                    each_slot(sides[1 - side] == block, one)
+                    return carry
+
+                pl.when(relaying[side])(lambda: lax.fori_loop(0, 3, forward, None))
+
+        def receive():
             def arrive(c, carry):
-                for side in range(3):
-                    (follow(side - 1, c) if side else direct(c)).wait_recv()
+                def wait(j):
+                    direct(c, j).wait_recv()
+                    follow(0, c, j).wait_recv()
+                    follow(1, c, j).wait_recv()
+
+                each_slot(s == block, wait)
 
                 def each(side, carry):
                     put(288 * side + 96 * c, 96)
+                    pl.when(k == 0)(lambda: hand(2 - side, 2 - c).start())
                     return carry
 
                 return lax.fori_loop(0, 3, each, carry)
 
-            lax.fori_loop(0, 3, arrive, 0)
-            for c in range(3):
-                direct(c).wait_send()
-                lead(0, c).wait_send()
-                lead(1, c).wait_send()
-
-        for side in range(2):
-
-            @pl.when(s == sides[side])
+            @pl.when(near_wall)
             def _():
-                for c in range(3):
-                    lead(side, c).wait_recv()
-                    follow(side, c).start()
-                for c in range(3):
-                    follow(side, c).wait_send()
-
-        @pl.when(in_after)
-        def _():
-            mirror[k, 1] = jnp.zeros((ROWS, LANES), F32)
-            lax.fori_loop(0, ROWS // 8, cut, 0, unroll=3)
-            for c in range(3):
-                lead_far(c).start()
-            for c in range(3):
-                follow_far(c).wait_recv()
-            put(0, ROWS)
-            for c in range(3):
-                lead_far(c).wait_send()
-
-        @pl.when(in_beyond)
-        def _():
-            for c in range(3):
-                lead_far(c).wait_recv()
-                follow_far(c).start()
-            for c in range(3):
-                follow_far(c).wait_send()
+                lax.fori_loop(0, 3, arrive, 0)
+
+                def sent(c, carry):
+                    each_slot(s == block, lambda j: ways(c, j, lambda copy: copy.wait_send()))
+                    return carry
+
+                lax.fori_loop(0, 3, sent, None)
+
+            for side in range(2):
+
+                def passed(c, carry):
+                    each_slot(sides[1 - side] == block, lambda j: follow(side, c, j).wait_send())
+                    return carry
+
+                pl.when(relaying[side])(lambda: lax.fori_loop(0, 3, passed, None))
+
+        return send, relays, receive
 
     def total(k, between):
         mine = pl.ds(2 * place.core, 2)
@@ -537,24 +552,13 @@
         for copy in [first, last] + outs:
             copy.wait_send()
 
-    def hand(g):
-        rows = pl.ds(288 * g, 288)
-        return remote(
-            states.at[0, pl.ds(2, 2), rows], halo.at[:, rows], halo_sem.at[0, g], halo_sem.at[1, g], place.down
-        )
-
-    early = jnp.logical_or(in_block, in_after)
     tell = remote(
         params.at[0, pl.ds(2 * place.pos, 2)], edge, esem.at[0], esem.at[1], place.down
     )
 
-    def hand_on():
-        for g in range(3):
-            hand(g).start()
-
     def middle():
         tell.start()
-        pl.when(jnp.logical_not(early))(hand_on)
+        pl.when(jnp.logical_not(near_wall))(hand_on)
 
         def own(l, carry):
             def load_row(row):
@@ -575,8 +579,9 @@
         lax.fori_loop(0, 3, later, 0)
         tell.wait_recv()
 
-        def chunk(g, carry):
-            hand(g).wait_recv()
+        def piece(i, carry):
+            c, g = 2 - i // 3, 2 - lax.rem(i, 3)
+            hand(g, c).wait_recv()
 
             def beside(l, carry):
                 def load_row(row):
@@ -585,16 +590,15 @@
                 def store_row(row, value):
                     field[l, at(row), :] = value
 
-                relax(
-                    place, load_row, store_row, edge, jnp.where(place.pos == 1, l, 1 - l), table, (g, g + 1)
-                )
+                layer = jnp.where(place.pos == 1, l, 1 - l)
+                relax(place, load_row, store_row, edge, layer, table, (g, g + 1), 4 * c, 4)
                 return carry
 
             lax.fori_loop(0, 2, beside, 0)
-            transport(place, field, states.at[1], (0, 1), g, 0, 12)
+            transport(place, field, states.at[1], (0, 1), g, 4 * c, 4)
             return carry
 
-        lax.fori_loop(0, 3, chunk, 0)
+        lax.fori_loop(0, 9, piece, 0)
 
     def last():
         def end(l, carry):
@@ -612,9 +616,15 @@
         lax.fori_loop(0, COLS, end, 0)
 
     def step(k, carry):
-        reflect(states.at[k], k)
-        moments(place, states.at[k], part, sums.at[k], z_sums)
-        total(k, lambda: pl.when(jnp.logical_and(early, k == 0))(hand_on))
+        send, relays, receive = reflect(states.at[k], k)
+        send()
+        moments(place, states.at[k], walls, part, sums.at[k], z_sums)
+
+        def between():
+            relays()
+
+        total(k, between)
+        receive()
         pl.when(k == 0)(middle)
         pl.when(k == 1)(last)
         return carry
@@ -622,7 +632,8 @@
     lax.fori_loop(0, 2, step, 0)
     tell.wait_send()
     for g in range(3):
-        hand(g).wait_send()
+        for c in range(3):
+            hand(g, c).wait_send()
 
 
 def first_call(x, mask):
@@ -673,7 +684,7 @@
             pltpu.VMEM((COLS + 2, ROWS, LANES), F32),
             pltpu.VMEM((2, 2, ROWS, LANES), F32),
             pltpu.VMEM((2, 2, ROWS, LANES), F32),
-            pltpu.VMEM((2, 2, 576, LANES), F32),
+            pltpu.VMEM((2, 2, 288, LANES), F32),
             pltpu.VMEM((COLS, 13, 8, LANES), F32),
             pltpu.VMEM((COLS, 10, 8, LANES), F32),
             pltpu.VMEM((2, COLS, 16, LANES), F32),
@@ -683,11 +694,11 @@
             pltpu.VMEM((2, 16, LANES), F32),
             pltpu.VMEM((3, 16, LANES), F32),
             dma,
-            dma((2, 3)),
             dma((2, 9)),
-            dma((2, 9)),
-            dma((2, 3)),
-            dma((2, 3)),
+            dma((2, 2, 9)),
+            dma((2, 2, 9)),
+            dma((2, 2, 3)),
+            dma((2, 2, 3)),
             dma((2, 2, 9)),
             dma((2,)),
         ],

time: 115 us -> 90.1 us (0.78)
  the two profiles are of different devices: /device:TPU:217 before, /device:TPU:1 now
where the time goes in v3:
time: 90.1 us; the launch traced here: 89.2 us
  Pallas kernels  87.1 us (97%)
  local copies, waits for them, and re-layouts  1.21 us (1%)
    pallas_call x1, Pallas kernels, second_call(): pl.pallas_call(functools.partial(second_kernel, block), out_shape=jax.Sha...  60.1 us
    pallas_call x1, Pallas kernels, first_call(): pl.pallas_call(first_kernel, out_shape=(jax.ShapeDtypeStruct((COLS, ROWS,...  27 us

profile of v3, /device:TPU:1, one launch (start us, length us, event | category | flops | bytes accessed | tf_op | source)
XLA Modules:
  0.0 89.2 jit_solution(7508920700762133738)
XLA Ops:
  0.0 27.0 %first.1 = (f32[4,864,128]{2,1,0:T(8,128)S(1)}, f32[8,128]{1,0:T(8,128)S(1)}, s32[1]{0:T(128)}) custom-call(f32[3456,128]{1,0:T(8,128)} %bitcast.34, s32[4,128]{1,0:T(4,128)} %mask_ref.1), custom_call_target="tpu_custom_call" | custom-call | tf_op jit(solution)/shard_map/first/pallas_call | solution.py:641
  27.7 60.3 %conditional.1 = (f32[864,4,128]{2,1,0:T(4,128)S(1)}) conditional(s32[]{:T(128)} %bitcast.17, (f32[4,864,128]{2,1,0:T(8,128)S(1)}, f32[8,128]{1,0:T(8,128)S(1)}) %tuple.69, (f32[4,864,128]{2,1,0:T(8,128)S(1)}, f32[8,128]{1,0:T(8,128)S(1)}) %tuple.69, (f32[4,864,128]{2,1,0:T(8,128)S(1)}, ...), branch_computations={%region_0.0_spmd, %region_1.0_spmd, %region_2.0_spmd, %region_3.0_... | conditional | bytes 8 | solution.py:716
  27.9 60.1 %second9.1 = f32[3456,128]{1,0:T(8,128)S(1)} custom-call(f32[4,864,128]{2,1,0:T(8,128)S(1)} %get-tuple-element.105.moved_ref, f32[8,128]{1,0:T(8,128)S(1)} %get-tuple-element.106.walls), custom_call_target="tpu_custom_call" | custom-call | tf_op jit(solution)/shard_map/cond/branch_9_fun/second9/pallas_call | solution.py:676
  88.0 1.2 %copy.36 = f32[864,4,128]{2,1,0:T(4,128)} copy(f32[864,4,128]{2,1,0:T(4,128)S(1)} %get-tuple-element.125) | data formatting | bytes 3538944
